TPU v7x, 256 devices: a whole 4x4x8 slice. The times are simulated.
256 devices in a mesh: dp: 16 (over z, y_hi), mp: 16 (over x, y_lo, core).
Axes of the slice: x: 4, y: 4 (y_hi: 2, y_lo: 2; y = y_hi * 2 + y_lo), z: 8, core: 2. Of those that a mesh axis runs over, the one named last changes fastest.
Arguments:
- tokens: bfloat16 [8192, 6144], P(('dp', 'mp')), may hold values from -24 to 24
- w_qkv: bfloat16 [6144, 32, 384], P(None, 'mp'), may hold values from -0.078125 to 0.078125
- w_out: bfloat16 [6144, 32, 128], P('dp', 'mp'), may hold values from -0.09375 to 0.09375
- grad_out: bfloat16 [8192, 6144], P(('dp', 'mp')), may hold values from -24 to 24
Outputs:
- grad_wqkv: bfloat16 [6144, 32, 384], P('dp', 'mp')
- grad_wout: bfloat16 [6144, 32, 128], P('dp', 'mp')
All inputs are finite; a program needn't handle non-finite values.
Results may differ from a plain program's by a relative error of at most 0.02.
Values may be sent and summed in bfloat16 or wider, within the bound.
A program may use at most 128 MiB of HBM per device.

v0:
```python
import jax
import jax.numpy as jnp
from jax import lax
from jax.sharding import PartitionSpec as P

PATCH = 256


def layer_norm(values):
    average = jnp.mean(values, axis=-1, keepdims=True)
    centred = values - average
    spread = jnp.mean(centred * centred, axis=-1, keepdims=True)
    return centred * lax.rsqrt(spread + 1e-06)


def body(tokens, w_qkv, w_out, grad_out):
    head_count = w_qkv.shape[1]
    head_size = w_out.shape[2]
    factor = head_size ** (-0.5)
    projected = jnp.einsum(
        "td,dhe->the",
        lax.all_gather(tokens, "mp", axis=0, tiled=True),
        w_qkv,
        preferred_element_type=jnp.float32,
    )
    row_count = projected.shape[0]
    images_here = row_count // PATCH
    query_raw = projected[..., :head_size]
    key_raw = projected[..., head_size : 2 * head_size]
    query_hat = layer_norm(query_raw).astype(jnp.bfloat16)
    key_hat = layer_norm(key_raw).astype(jnp.bfloat16)
    value_hat = projected[..., 2 * head_size :].astype(jnp.bfloat16)

    def blocks(values):
        return values.reshape(images_here, PATCH, head_count, head_size)

    def unblock(values):
        return values.reshape(row_count, head_count, head_size)

    scores = (
        jnp.einsum(
            "iqhe,ikhe->ihqk",
            blocks(query_hat),
            blocks(key_hat),
            preferred_element_type=jnp.float32,
        )
        * factor
    )
    weights = jnp.exp(scores)
    chances = weights / jnp.sum(weights, axis=-1, keepdims=True)
    chances_low = chances.astype(jnp.bfloat16)
    context = unblock(
        jnp.einsum(
            "ihqk,ikhe->iqhe", chances_low, blocks(value_hat), preferred_element_type=jnp.float32
        )
    ).astype(jnp.bfloat16)
    gathered, grad_full = (
        lax.all_gather(tokens, "mp", axis=0, tiled=True),
        lax.all_gather(grad_out, "mp", axis=0, tiled=True),
    )
    grad_context = jnp.einsum(
        "td,dhe->the",
        grad_full,
        lax.all_gather(w_out, "dp", axis=0, tiled=True),
        preferred_element_type=jnp.float32,
    ).astype(jnp.bfloat16)
    grad_chances = jnp.einsum(
        "iqhe,ikhe->ihqk",
        blocks(grad_context),
        blocks(value_hat),
        preferred_element_type=jnp.float32,
    )
    grad_value = unblock(
        jnp.einsum(
            "ihqk,iqhe->ikhe", chances_low, blocks(grad_context), preferred_element_type=jnp.float32
        )
    )
    grad_scores = (
        chances * (grad_chances - jnp.sum(chances * grad_chances, axis=-1, keepdims=True)) * factor
    )
    scores_low = grad_scores.astype(jnp.bfloat16)
    grad_qhat = unblock(
        jnp.einsum(
            "ihqk,ikhe->iqhe", scores_low, blocks(key_hat), preferred_element_type=jnp.float32
        )
    )
    grad_khat = unblock(
        jnp.einsum(
            "ihqk,iqhe->ikhe", scores_low, blocks(query_hat), preferred_element_type=jnp.float32
        )
    )
    grad_query = jax.vjp(layer_norm, query_raw)[1](grad_qhat)[0]
    grad_key = jax.vjp(layer_norm, key_raw)[1](grad_khat)[0]
    grad_proj = jnp.concatenate([grad_query, grad_key, grad_value], axis=-1).astype(jnp.bfloat16)
    term_qkv = jnp.einsum("td,the->dhe", gathered, grad_proj, preferred_element_type=jnp.float32)
    term_out = jnp.einsum("td,the->dhe", grad_full, context, preferred_element_type=jnp.float32)
    summed = lax.psum_scatter(
        jnp.concatenate([term_qkv, term_out], axis=2).astype(jnp.bfloat16),
        "dp",
        scatter_dimension=0,
        tiled=True,
    ).astype(jnp.float32)
    return (
        summed[..., : 3 * head_size].astype(jnp.bfloat16),
        summed[..., 3 * head_size :].astype(jnp.bfloat16),
    )


def solution(mesh):
    return jax.shard_map(
        body,
        mesh=mesh,
        in_specs=(
            P(("dp", "mp"), None),
            P(None, "mp", None),
            P("dp", "mp", None),
            P(("dp", "mp"), None),
        ),
        out_specs=(P("dp", "mp", None), P("dp", "mp", None)),
        check_vma=False,
    )
```

profile of v0, /device:TPU:8, one launch (start us, length us, event | category | flops | bytes accessed | tf_op | source)
XLA Modules:
  0.0 517.7 jit_solution(12761866212270962388)
XLA Ops:
  7.2 0.0 all-gather.4.cloned.1.call-start
  7.2 0.7 all-gather.4.cloned.1.call-update
  7.9 0.0 all-gather.8.cloned.1.call-start
  7.9 1.6 copy.51
  9.6 0.0 all-gather.8.cloned.1.call-update
  9.6 0.0 all-gather.6.cloned.1.call-start
  9.6 0.7 all-gather.6.cloned.1.call-update
  10.3 0.0 reduce-scatter.4.cloned.1.call-start
  10.4 47.1 %all-gather.4.cloned.1.call-done = bf16[512,6144]{1,0:T(8,128)(2,1)} async-done(((bf16[32,6144]{1,0:T(8,128)(2,1)}), bf16[512,6144]{1,0:T(8,128)(2,1)}) %all-gather.4.cloned.1.call-update) | async-done | bytes 6291472 | tf_op jit(solution)/shard_map/all_gather | solution.py:58
  57.5 9.4 %fusion.1 = f32[512,2,384]{2,0,1:T(8,128)S(1)} fusion(bf16[6144,2,384]{2,1,0:T(2,128)(2,1)} %param.5, bf16[512,6144]{1,0:T(8,128)(2,1)} %all-gather.4.cloned.1.call-done), kind=kOutput, calls=%fused_computation.3 | convolution fusion | flops 4831838208 | bytes 17301504 | tf_op jit(solution)/shard_map/td,dhe->the/dot_general | solution.py:20
  66.9 0.4 slice_reduce_fusion
  67.3 0.6 multiply_reduce_fusion.1
  68.0 0.6 multiply_convert_fusion
  68.6 1.4 fusion.32
  70.0 0.3 fusion.13
  70.3 83.7 %all-gather.8.cloned.1.call-done = bf16[6144,2,128]{2,0,1:T(8,128)(2,1)} async-done(((bf16[384,2,128]{2,0,1:T(8,128)(2,1)}), bf16[6144,2,128]{2,0,1:T(8,128)(2,1)}) %all-gather.8.cloned.1.call-update) | async-done | bytes 3145744 | tf_op jit(solution)/shard_map/all_gather | solution.py:64
  154.0 44.1 %all-gather.6.cloned.1.call-done = bf16[512,6144]{1,0:T(8,128)(2,1)} async-done(((bf16[32,6144]{1,0:T(8,128)(2,1)}), bf16[512,6144]{1,0:T(8,128)(2,1)}) %all-gather.6.cloned.1.call-update) | async-done | bytes 6291472 | tf_op jit(solution)/shard_map/all_gather | solution.py:59
  198.1 6.2 %fusion.15 = bf16[512,2,128]{2,0,1:T(8,128)(2,1)} fusion(bf16[6144,2,128]{2,0,1:T(8,128)(2,1)} %all-gather.8.cloned.1.call-done, bf16[512,6144]{1,0:T(8,128)(2,1)} %all-gather.6.cloned.1.call-done), kind=kOutput, calls=%fused_computation.21 | convolution fusion | flops 1610743808 | bytes 9699328 | tf_op jit(solution)/shard_map/td,dhe->the/dot_general | solution.py:61
  204.3 2.0 fusion.18
  206.4 1.0 fusion.19
  207.4 1.2 fusion.40
  208.7 2.9 convolution_bitcast_fusion.1
  211.5 2.9 convolution_bitcast_fusion
  214.5 1.1 copy.66
  215.6 1.1 copy.62
  216.7 1.2 copy.59
  218.0 1.2 copy.56
  219.2 0.4 fusion.30
  219.6 1.1 fusion.46
  220.8 0.6 fusion.47
  221.4 0.0 slice-start
  221.4 1.3 add_convert_fusion.1
  222.8 0.0 slice-start.1
  222.8 4.8 fusion.4
  227.6 0.0 slice-done
  227.6 0.0 slice-done.1
  227.6 5.6 %fusion.3 = bf16[6144,2,384]{0,2,1:T(8,128)(2,1)S(1)} fusion(bf16[512,6144]{1,0:T(8,128)(2,1)S(1)} %bitcast.75, bf16[512,2,128]{2,0,1:T(8,128)(2,1)S(1)} %bitcast.71, bf16[512,2,128]{2,0,1:T(8,128)(2,1)S(1)} %get-tuple-element.15, bf16[512,2,128]{2,0,1:T(8,128)(2,1)S(1)} %get-tuple-element.14), kind=kOutput, calls=%fused_computation.5 | convolution fusion | flops 4838916096 | bytes 16515072 | tf_op jit(solution)/shard_map/td,the->dhe/dot_general | solution.py:95
  233.2 5.0 pad_maximum_fusion
  238.2 16.6 %copy.86 = bf16[6144,1024]{1,0:T(8,128)(2,1)} copy(bf16[6144,1024]{0,1:T(8,128)(2,1)} %bitcast.59) | data formatting | bytes 25165824
  254.8 0.0 reduce-scatter.4.cloned.1.call-update
  254.9 252.1 %reduce-scatter.4.cloned.1.call-done = bf16[384,1024]{1,0:T(8,128)(2,1)} async-done(((bf16[6144,1024]{1,0:T(8,128)(2,1)}), bf16[384,1024]{1,0:T(8,128)(2,1)}) %reduce-scatter.4.cloned.1.call-update) | async-done | bytes 786448
  506.9 1.5 copy.87
  508.5 0.1 slice.26
  508.5 1.8 copy.68
  510.3 0.9 copy.69
  (10 shorter events, 0.1 us)
Async XLA Ops:
  7.2 50.4 %all-gather.4.cloned.1.call-start = ((), (), s32[]{:S(2)}) async-start(), calls=%async_computation.1 | async-start | bytes 6684672 | tf_op jit(solution)/shard_map/all_gather | solution.py:58
  7.9 146.1 %all-gather.8.cloned.1.call-start = ((), (), s32[]{:S(2)}) async-start(), calls=%async_computation.3 | async-start | bytes 3342336 | tf_op jit(solution)/shard_map/all_gather | solution.py:64
  9.6 188.5 %all-gather.6.cloned.1.call-start = ((), (), s32[]{:S(2)}) async-start(), calls=%async_computation.2 | async-start | bytes 6684672 | tf_op jit(solution)/shard_map/all_gather | solution.py:59
  10.3 496.6 %reduce-scatter.4.cloned.1.call-start = ((), (), s32[]{:S(2)}) async-start(), calls=%async_computation.4 | async-start | bytes 13369344
  221.4 6.1 %slice-start = ((s8[6291456]{0:T(1024)(128)(4,1)}), s8[4194304]{0:T(1024)(128)(4,1)S(1)}, s32[]{:S(2)}) async-start(s8[6291456]{0:T(1024)(128)(4,1)} %bitcast.74), calls=%async_computation.5 | async-start | bytes 8388608
  222.8 4.8 slice-start.1
Sparse Core Ops, SparseCore 0:
  9.8 47.6 all-gather.3
  60.7 93.2 all-gather.7
  155.9 42.2 all-gather.5
  255.0 251.9 reduce-scatter.3
where the time goes:
time: 520 us; the launch traced here: 518 us
  waiting for transfers between devices  428 us (82%)
  matrix products  37.7 us (7%)
  local copies, waits for them, and re-layouts  27.2 us (5%)
  between operations  14 us (3%)
  other arithmetic  10.2 us (2%)
    unnamed x5, waiting for transfers between devices  253 us
    all_gather x1, waiting for transfers between devices, body(): lax.all_gather(w_out, 'dp', axis=0, tiled=True)  83.7 us
    all_gather x1, waiting for transfers between devices, body(): lax.all_gather(tokens, 'mp', axis=0, tiled=True)  47.1 us
    all_gather x1, waiting for transfers between devices, body(): lax.all_gather(grad_out, 'mp', axis=0, tiled=True)  44.1 us
    unnamed x9, local copies, waits for them, and re-layouts  22.4 us
  transfers between devices with their start and end apart: 4, of which 4 were waited for; matrix products, arithmetic and copies ran while one was open for 3% of the time, Pallas kernels for 0%

commit v1 on v0

v1 whole, which is shorter than its diff:
```python
import jax
import jax.numpy as jnp
from jax import lax
from jax.experimental import pallas as pl
from jax.experimental.pallas import tpu as pltpu
from jax.sharding import PartitionSpec as P

MESH = pl.DeviceIdType.MESH
F32 = jnp.float32
BF16 = jnp.bfloat16

NX, NZ = 4, 8
BLOCK = 32
PATCH = 256
WIDTH = 6144
SPAN = 384
PAIR = 2 * SPAN
ROUNDS = 2 * NZ
HD = 128
EPS = 1e-06
FACTOR = HD ** (-0.5)


def dot(a, b, dims):
    return lax.dot_general(a, b, (dims, ((), ())), preferred_element_type=F32)


def centre(values):
    centred = values - jnp.mean(values, axis=-1, keepdims=True)
    spread = jnp.mean(centred * centred, axis=-1, keepdims=True)
    return centred, lax.rsqrt(spread + EPS)


def norm_grad(centred, scale, grad):
    slope = jnp.mean(grad * centred, axis=-1, keepdims=True) * (scale * scale * scale)
    inner = grad * scale - centred * slope
    return inner - jnp.mean(inner, axis=-1, keepdims=True)


def kernel(
    tok_ref, wq_ref, wo_ref, go_ref,
    oq_ref, oc_ref,
    rows, extra, wq, wo, wpart, proj, gctx, hats, chances, bt, run, first,
    local, g_send, g_recv, w_send, w_recv, y_send, y_recv, b_send, b_recv, r_send, r_recv,
):
    dp, mp = lax.axis_index("dp"), lax.axis_index("mp")
    z, yh = dp // 2, dp % 2
    x, yl, core = mp // 4, (mp // 2) % 2, mp % 2

    def place(z_, yh_, x_, yl_, core_):
        return (z_ * 2 + yh_, x_ * 4 + yl_ * 2 + core_)

    right_x, left_x, far_x = (x + 1) % NX, (x + 3) % NX, (x + 2) % NX
    pair = place(z, yh, x, 1 - yl, core)
    right = place(z, yh, right_x, yl, core)
    left = place(z, yh, left_x, yl, core)
    sibling = place(z, yh, x, yl, 1 - core)
    outer = place(z, 1 - yh, x, 1 - yl, core)
    across = place(z, 1 - yh, x, yl, core)
    up = place((z + 1) % NZ, yh, x, yl, core)
    down = place((z + 7) % NZ, yh, x, yl, core)
    sides = (up, down)

    def remote(src, dst, send, recv, to):
        return pltpu.make_async_remote_copy(
            src_ref=src, dst_ref=dst, send_sem=send, recv_sem=recv, device_id=to, device_id_type=MESH
        )

    barrier = pltpu.get_barrier_semaphore()
    for to in (pair, right, left, sibling, outer, across, up, down):
        pl.semaphore_signal(barrier, inc=1, device_id=to, device_id_type=MESH)

    mine = x * 2 + yl
    loads = (
        pltpu.make_async_copy(tok_ref, rows.at[0, mine, core], local.at[0]),
        pltpu.make_async_copy(go_ref, rows.at[1, mine, core], local.at[1]),
        pltpu.make_async_copy(wo_ref, wo.at[z, yh], local.at[2]),
        pltpu.make_async_copy(wq_ref, wq, local.at[3]),
    )
    for load in loads:
        load.start()
    proj[...] = jnp.zeros_like(proj)
    gctx[...] = jnp.zeros_like(gctx)
    for load in loads[:3]:
        load.wait()
    pl.semaphore_wait(barrier, 8)


    def target(r):
        j = r % NZ
        step = NZ // 2 - (j + 1) // 2
        return (z + jnp.where(j % 2 == 1, step, NZ - step)) % NZ

    def columns(r):
        return pl.ds(pl.multiple_of(target(r) * PAIR, PAIR), PAIR)

    def block(r, bx, by):
        return rows.at[r // NZ, bx * 2 + by, core, :, columns(r)]

    def move(r, slot, bx, by, to):
        part = block(r, bx, by)
        return remote(part, part, g_send.at[r, slot], g_recv.at[r, slot], to)

    def landed(r, slot, bx, by):
        move(r, slot, bx, by, pair).wait_recv()

    def swap(r, lane):
        part = rows.at[r // NZ, :, lane, :, columns(r)]
        return remote(part, part, g_send.at[r, 7], g_recv.at[r, 7], sibling)

    def lend(r):
        cols = pl.ds(pl.multiple_of(target(r) * PAIR + (1 - yh) * SPAN, SPAN), SPAN)
        there = pl.ds(pl.multiple_of(target(r) * SPAN, SPAN), SPAN)
        half = pl.ds(core * 4, 4)
        return remote(
            rows.at[r // NZ, half, :, :, cols], extra.at[r // NZ, half, :, :, there],
            g_send.at[r, 8], g_recv.at[r, 8], outer,
        )

    def share(r, owner):
        there = pl.ds(pl.multiple_of(target(r) * SPAN, SPAN), SPAN)
        part = extra.at[r // NZ, pl.ds(owner * 4, 4), :, :, there]
        return remote(part, part, g_send.at[r, 9], g_recv.at[r, 9], sibling)


    def weights(side, m):
        hop = m // 2
        from_z = (z + (NZ - hop if side == 0 else hop)) % NZ
        own = (m % 2 == 0) if (m < 6 or side == 0) else False
        part = wo.at[from_z, yh if own else 1 - yh]
        return remote(part, part, w_send.at[side, m], w_recv.at[side, m], sides[side])

    def weights_landed(m):
        for side in range(2):
            weights(side, m).wait_recv()

    def weights_across():
        part = wo.at[z, yh]
        return remote(part, part, y_send.at[0], y_recv.at[0], across)

    def send_weights(m):
        if m == 1:
            weights_across().wait_recv()
        if m >= 2:
            weights_landed(m - 2)
        if m == 6:
            weights_landed(5)
        for side in range(2):
            weights(side, m).start()


    def image_rows(i):
        return pl.ds(pl.multiple_of(i * PATCH, PATCH), PATCH)

    def head_part(i, h, part):
        return proj[image_rows(i), pl.ds(pl.multiple_of((h * 3 + part) * HD, HD), HD)]

    def sums(g, h):
        return pl.ds(pl.multiple_of((g * 2 + h) * HD, HD), HD)

    def hand_over(g, n):
        i, h = n // 2, n % 2
        return remote(
            bt.at[0, sums(g, h), image_rows(i)], bt.at[1, sums(g, h), image_rows(i)],
            b_send.at[g, n], b_recv.at[g, n], across,
        )

    def forward(n):
        i, h = n // 2, n % 2
        centred_q, scale_q = centre(head_part(i, h, 0))
        centred_k, scale_k = centre(head_part(i, h, 1))
        query_hat = (centred_q * scale_q).astype(BF16)
        key_hat = (centred_k * scale_k).astype(BF16)
        value_hat = head_part(i, h, 2).astype(BF16)
        hats[n, 0] = query_hat
        hats[n, 1] = key_hat
        weight = jnp.exp(dot(query_hat, key_hat, ((1,), (1,))) * FACTOR)
        chance = weight / jnp.sum(weight, axis=-1, keepdims=True)
        chances[n] = chance
        context = dot(chance.astype(BF16), value_hat, ((1,), (0,)))
        bt[0, sums(3, h), image_rows(i)] = context.T.astype(BF16)
        hand_over(3, n).start()

    def backward(n):
        i, h = n // 2, n % 2
        chance = chances[n]
        chance_low = chance.astype(BF16)
        query_hat, key_hat = hats[n, 0], hats[n, 1]
        value_hat = head_part(i, h, 2).astype(BF16)
        grad_context = gctx[image_rows(i), pl.ds(pl.multiple_of(h * HD, HD), HD)].astype(BF16)
        grad_value = dot(chance_low, grad_context, ((0,), (0,)))
        bt[0, sums(0, h), image_rows(i)] = grad_value.T.astype(BF16)
        hand_over(0, n).start()
        grad_chance = dot(grad_context, value_hat, ((1,), (1,)))
        inner = jnp.sum(chance * grad_chance, axis=-1, keepdims=True)
        grad_score = (chance * (grad_chance - inner) * FACTOR).astype(BF16)
        grad_qhat = dot(grad_score, key_hat, ((1,), (0,)))
        grad_khat = dot(grad_score, query_hat, ((0,), (0,)))
        grad_key = norm_grad(*centre(head_part(i, h, 1)), grad_khat)
        bt[0, sums(1, h), image_rows(i)] = grad_key.T.astype(BF16)
        grad_query = norm_grad(*centre(head_part(i, h, 0)), grad_qhat)
        bt[0, sums(2, h), image_rows(i)] = grad_query.T.astype(BF16)

    def gathered(r):
        return rows[r // NZ, :, :, :, columns(r)].reshape(2 * PATCH, PAIR)

    def project(r):
        base = target(r) * PAIR

        @pl.loop(0, PAIR // HD)
        def _(k):
            here = pl.ds(pl.multiple_of(k * HD, HD), HD)
            wpart[here, :] = wq[pl.ds(pl.multiple_of(base + k * HD, HD), HD)].reshape(HD, 6 * HD)

        proj[...] += dot(gathered(r), wpart[...], ((1,), (0,)))

    def project_back(r):
        @pl.loop(0, PAIR // HD)
        def _(k):
            here = pl.ds(pl.multiple_of(k * HD, HD), HD)
            there = pl.ds(pl.multiple_of((k % 3) * HD, HD), HD)
            wpart[here, pl.ds(0, 2 * HD)] = wo[target(r), k // 3, there].reshape(HD, 2 * HD)

        gctx[...] += dot(gathered(r), wpart[:, pl.ds(0, 2 * HD)], ((1,), (0,)))

    weights_across().start()
    send_weights(0)

    @pl.loop(0, ROUNDS + 4)
    def _(it):
        @pl.when(it < ROUNDS)
        def _():
            move(it, 0, x, yl, pair).start()
            move(it, 1, x, yl, right).start()
            move(it, 2, x, yl, left).start()

        for m, when in ((1, 2), (2, 3), (3, 5), (4, 7), (5, 8), (6, 11)):

            @pl.when(it == when)
            def _(m=m):
                send_weights(m)

        @pl.when((it >= 1) & (it < ROUNDS + 1))
        def _():
            r = it - 1
            landed(r, 0, x, 1 - yl)
            move(r, 3, x, 1 - yl, right).start()
            move(r, 4, x, 1 - yl, left).start()
            landed(r, 1, left_x, yl)
            landed(r, 2, right_x, yl)
            onward = place(z, yh, jnp.where(core == 0, right_x, left_x), yl, core)
            move(r, 5, jnp.where(core == 0, left_x, right_x), yl, onward).start()

        @pl.when((it >= 2) & (it < ROUNDS + 2))
        def _():
            r = it - 2
            landed(r, 5, far_x, yl)
            move(r, 6, far_x, yl, pair).start()

        @pl.when((it >= 3) & (it < ROUNDS + 3))
        def _():
            r = it - 3
            landed(r, 3, left_x, 1 - yl)
            landed(r, 4, right_x, 1 - yl)
            landed(r, 6, far_x, 1 - yl)
            swap(r, core).start()

        @pl.when(it == 4)
        def _():
            loads[3].wait()

        @pl.when(it == 12)
        def _():
            weights_landed(6)

        @pl.when((it >= 4) & (it < NZ + 4))
        def _():
            r = it - 4
            swap(r, 1 - core).wait_recv()
            lend(r).start()
            project(r)

        @pl.when(it >= NZ + 4)
        def _():
            r = it - 4
            swap(r, 1 - core).wait_recv()
            project_back(r)

            @pl.when(it < NZ + 8)
            def _():
                forward(it - NZ - 4)

    @pl.loop(0, NZ)
    def _(r):
        lend(r).wait_recv()
        share(r, core).start()

    @pl.loop(0, 4)
    def _(n):
        backward(n)

    @pl.loop(0, 4)
    def _(n):
        hand_over(1, n).start()

    @pl.loop(0, 4)
    def _(n):
        hand_over(2, n).start()

    @pl.loop(NZ, ROUNDS)
    def _(r):
        lend(r).start()

    @pl.loop(0, NZ)
    def _(r):
        share(r, 1 - core).wait_recv()


    def term(g, to_z):
        a = g // 3
        own_cols = pl.ds(pl.multiple_of(to_z * PAIR + yh * SPAN, SPAN), SPAN)
        other_cols = pl.ds(pl.multiple_of(to_z * SPAN, SPAN), SPAN)
        here = pl.ds(pl.multiple_of(g * 2 * HD, 2 * HD), 2 * HD)
        own = rows[a, :, :, :, own_cols].reshape(2 * PATCH, SPAN)
        other = extra[a, :, :, :, other_cols].reshape(2 * PATCH, SPAN)
        return dot(bt[0, here, :], own, ((1,), (0,))) + dot(bt[1, here, :], other, ((1,), (0,)))

    def pass_on(side, s, g, h):
        source = first.at[sums(g, h)] if s == 0 else run.at[side, s - 1, sums(g, h)]
        return remote(
            source, run.at[side, s, sums(g, h)],
            r_send.at[side, s, g * 2 + h], r_recv.at[side, s, g * 2 + h], sides[side],
        )

    def finish(g):
        total = term(g, z)
        for h in range(2):
            part = total[h * HD : (h + 1) * HD]
            for side in range(2):
                pass_on(side, 3, g, h).wait_recv()
                part = part + run[side, 3, sums(g, h)].astype(F32)
            done = part.T.astype(BF16)

            @pl.when(g < 3)
            def _():
                oq_ref[:, pl.ds(pl.multiple_of((h * 3 + 2 - g) * HD, HD), HD)] = done

            @pl.when(g == 3)
            def _():
                oc_ref[:, h * HD : (h + 1) * HD] = done

    @pl.loop(0, 4)
    def _(g):
        @pl.when(g == 3)
        def _():
            @pl.loop(NZ, ROUNDS)
            def _(r):
                share(r, 1 - core).wait_recv()

        @pl.loop(0, 4)
        def _(n):
            hand_over(g, n).wait_recv()

        start = term(g, (z + 4) % NZ)
        for h in range(2):
            first[sums(g, h)] = start[h * HD : (h + 1) * HD].astype(BF16)
            pass_on(h, 0, g, h).start()
        for s in range(1, 4):
            for side in range(2):
                part = term(g, (z + (4 - s if side == 0 else 4 + s)) % NZ)
                for h in (0, 1) if (s > 1 or side == 1) else (1, 0):
                    piece = part[h * HD : (h + 1) * HD]
                    if s > 1 or h == side:
                        pass_on(side, s - 1, g, h).wait_recv()
                        piece = piece + run[side, s - 1, sums(g, h)].astype(F32)
                    run[side, s - 1, sums(g, h)] = piece.astype(BF16)
                    pass_on(side, s, g, h).start()
            if s == 1:

                @pl.when(g > 0)
                def _():
                    finish(g - 1)

        @pl.when(g == 1)
        def _():
            @pl.loop(NZ, ROUNDS)
            def _(r):
                lend(r).wait_recv()
                share(r, core).start()

    finish(3)


    weights_across().wait_send()
    for side in range(2):
        for m in range(7):
            weights(side, m).wait_send()

    @pl.loop(0, ROUNDS)
    def _(r):
        for slot in range(7):
            move(r, slot, x, yl, pair).wait_send()
        swap(r, core).wait_send()
        lend(r).wait_send()
        share(r, core).wait_send()

    @pl.loop(0, 4)
    def _(g):
        for n in range(4):
            hand_over(g, n).wait_send()
        for side in range(2):
            for s in range(4):
                for h in range(2):
                    if s > 0 or h == side:
                        pass_on(side, s, g, h).wait_send()


def body(tokens, w_qkv, w_out, grad_out):
    dma = pltpu.SemaphoreType.DMA
    vmem = pltpu.VMEM
    grad_qkv, grad_wo = pl.pallas_call(
        kernel,
        out_shape=(
            jax.ShapeDtypeStruct((SPAN, 6 * HD), BF16),
            jax.ShapeDtypeStruct((SPAN, 2 * HD), BF16),
        ),
        in_specs=[pl.BlockSpec(memory_space=pl.ANY)] * 4,
        out_specs=(pl.BlockSpec(memory_space=vmem), pl.BlockSpec(memory_space=vmem)),
        scratch_shapes=[
            vmem((2, 8, 2, BLOCK, WIDTH), BF16),
            vmem((2, 8, 2, BLOCK, WIDTH // 2), BF16),
            vmem((WIDTH, 2, 3 * HD), BF16),
            vmem((NZ, 2, SPAN, 2, HD), BF16),
            vmem((PAIR, 6 * HD), BF16),
            vmem((2 * PATCH, 6 * HD), F32),
            vmem((2 * PATCH, 2 * HD), F32),
            vmem((4, 2, PATCH, HD), BF16),
            vmem((4, PATCH, PATCH), F32),
            vmem((2, 8 * HD, 2 * PATCH), BF16),
            vmem((2, 4, 8 * HD, SPAN), BF16),
            vmem((8 * HD, SPAN), BF16),
            dma((4,)),
            dma((ROUNDS, 10)), dma((ROUNDS, 10)),
            dma((2, 7)), dma((2, 7)),
            dma((1,)), dma((1,)),
            dma((4, 4)), dma((4, 4)),
            dma((2, 4, 8)), dma((2, 4, 8)),
        ],
        compiler_params=pltpu.CompilerParams(
            collective_id=0, has_side_effects=True, vmem_limit_bytes=60 << 20
        ),
    )(tokens, w_qkv, w_out, grad_out)
    return grad_qkv.reshape(SPAN, 2, 3 * HD), grad_wo.reshape(SPAN, 2, HD)


def solution(mesh):
    return jax.shard_map(
        body,
        mesh=mesh,
        in_specs=(
            P(("dp", "mp"), None),
            P(None, "mp", None),
            P("dp", "mp", None),
            P(("dp", "mp"), None),
        ),
        out_specs=(P("dp", "mp", None), P("dp", "mp", None)),
        check_vma=False,
    )
```

time: 520 us -> 177 us (0.34)
  waiting for transfers between devices: 428 us -> 0 us
  Pallas kernels: 0 us -> 172 us
  matrix products: 37.7 us -> 0 us
  local copies, waits for them, and re-layouts: 27.2 us -> 4.16 us
  between operations: 14 us -> 0.64 us
  other arithmetic: 10.2 us -> 0 us
    unnamed x5 -> x0, waiting for transfers between devices: 253 us -> none
    all_gather x3 -> x0, waiting for transfers between devices: 175 us -> none  [the longest x1 83.7 us: body(): lax.all_gather(w_out, 'dp', axis=0, tiled=True)]
    pallas_call x0 -> x1, Pallas kernels: none -> 172 us  [body(): pl.pallas_call(kernel, out_shape=(jax.ShapeDtypeStruct((SPAN, 6 * HD), BF...]
    dot_general x10 -> x0, matrix products: 36.3 us -> none  [the longest x1 9.36 us: body(): jnp.einsum('td,dhe->the', lax.all_gather(tokens, 'mp', axis=0, tiled=True...]
    unnamed x9 -> x0, local copies, waits for them, and re-layouts: 22.4 us -> none
  transfers between devices with their start and end apart: 4 -> 0, of which waited for: 4 -> 0; matrix products, arithmetic and copies ran while one was open for 3% -> 0% of each run, Pallas kernels for 0% -> 0%
where the time goes in v1:
time: 177 us; the launch traced here: 176 us
  Pallas kernels  172 us (97%)
  local copies, waits for them, and re-layouts  4.16 us (2%)
    pallas_call x1, Pallas kernels, body(): pl.pallas_call(kernel, out_shape=(jax.ShapeDtypeStruct((SPAN, 6 * HD), BF...  172 us
    reshape x2, local copies, waits for them, and re-layouts, body(): return (grad_qkv.reshape(SPAN, 2, 3 * HD), grad_wo.reshape(SPAN, 2, HD))  4.16 us

profile of v1, /device:TPU:8, one launch (start us, length us, event | category | flops | bytes accessed | tf_op | source)
XLA Modules:
  0.0 176.4 jit_solution(532385385494561500)
XLA Ops:
  0.6 171.6 %shard_map.59 = (bf16[384,768]{1,0:T(8,128)(2,1)}, bf16[384,256]{1,0:T(8,128)(2,1)}) custom-call(bf16[32,6144]{1,0:T(8,128)(2,1)} %tok_ref.1, bf16[6144,2,384]{2,1,0:T(2,128)(2,1)} %wq_ref.1, bf16[384,2,128]{2,1,0:T(2,128)(2,1)} %wo_ref.1, bf16[32,6144]{1,0:T(8,128)(2,1)} %go_ref.1), custom_call_target="tpu_custom_call" | custom-call | tf_op jit(solution)/shard_map/pallas_call | solution.py:421
  172.2 2.5 %reshape.10 = bf16[384,2,384]{2,1,0:T(2,128)(2,1)} reshape(bf16[384,768]{1,0:T(8,128)(2,1)} %get-tuple-element.4) | data formatting | bytes 1179648 | tf_op jit(solution)/shard_map/reshape | solution.py:453
  174.7 1.7 reshape.11

commit v2 on v1

--- a/solution.py
+++ b/solution.py
@@ -113,13 +113,31 @@
         there = pl.ds(pl.multiple_of(target(r) * SPAN, SPAN), SPAN)
         half = pl.ds(core * 4, 4)
         return remote(
-            rows.at[r // NZ, half, :, :, cols], extra.at[r // NZ, half, :, :, there],
+            rows.at[0, half, :, :, cols], extra.at[0, half, :, :, there],
             g_send.at[r, 8], g_recv.at[r, 8], outer,
         )
 
     def share(r, owner):
         there = pl.ds(pl.multiple_of(target(r) * SPAN, SPAN), SPAN)
-        part = extra.at[r // NZ, pl.ds(owner * 4, 4), :, :, there]
+        part = extra.at[0, pl.ds(owner * 4, 4), :, :, there]
+        return remote(part, part, g_send.at[r, 9], g_recv.at[r, 9], sibling)
+
+    def quarter(r, bx):
+        there = pl.ds(pl.multiple_of(target(r) * SPAN, SPAN), SPAN)
+        return extra.at[1, pl.ds(bx * 2, 2), core, :, there]
+
+    def give(r):
+        cols = pl.ds(pl.multiple_of(target(r) * PAIR + (1 - yh) * SPAN, SPAN), SPAN)
+        mine = rows.at[1, pl.ds(x * 2, 2), core, :, cols]
+        return remote(mine, quarter(r, x), g_send.at[r, 8], g_recv.at[r, 8], outer)
+
+    def pass_quarter(r, slot, bx, to):
+        part = quarter(r, bx)
+        return remote(part, part, g_send.at[r, slot], g_recv.at[r, slot], to)
+
+    def swap_quarters(r, lane):
+        there = pl.ds(pl.multiple_of(target(r) * SPAN, SPAN), SPAN)
+        part = extra.at[1, :, lane, :, there]
         return remote(part, part, g_send.at[r, 9], g_recv.at[r, 9], sibling)
 
 
@@ -223,98 +241,6 @@
 
         gctx[...] += dot(gathered(r), wpart[:, pl.ds(0, 2 * HD)], ((1,), (0,)))
 
-    weights_across().start()
-    send_weights(0)
-
-    @pl.loop(0, ROUNDS + 4)
-    def _(it):
-        @pl.when(it < ROUNDS)
-        def _():
-            move(it, 0, x, yl, pair).start()
-            move(it, 1, x, yl, right).start()
-            move(it, 2, x, yl, left).start()
-
-        for m, when in ((1, 2), (2, 3), (3, 5), (4, 7), (5, 8), (6, 11)):
-
-            @pl.when(it == when)
-            def _(m=m):
-                send_weights(m)
-
-        @pl.when((it >= 1) & (it < ROUNDS + 1))
-        def _():
-            r = it - 1
-            landed(r, 0, x, 1 - yl)
-            move(r, 3, x, 1 - yl, right).start()
-            move(r, 4, x, 1 - yl, left).start()
-            landed(r, 1, left_x, yl)
-            landed(r, 2, right_x, yl)
-            onward = place(z, yh, jnp.where(core == 0, right_x, left_x), yl, core)
-            move(r, 5, jnp.where(core == 0, left_x, right_x), yl, onward).start()
-
-        @pl.when((it >= 2) & (it < ROUNDS + 2))
-        def _():
-            r = it - 2
-            landed(r, 5, far_x, yl)
-            move(r, 6, far_x, yl, pair).start()
-
-        @pl.when((it >= 3) & (it < ROUNDS + 3))
-        def _():
-            r = it - 3
-            landed(r, 3, left_x, 1 - yl)
-            landed(r, 4, right_x, 1 - yl)
-            landed(r, 6, far_x, 1 - yl)
-            swap(r, core).start()
-
-        @pl.when(it == 4)
-        def _():
-            loads[3].wait()
-
-        @pl.when(it == 12)
-        def _():
-            weights_landed(6)
-
-        @pl.when((it >= 4) & (it < NZ + 4))
-        def _():
-            r = it - 4
-            swap(r, 1 - core).wait_recv()
-            lend(r).start()
-            project(r)
-
-        @pl.when(it >= NZ + 4)
-        def _():
-            r = it - 4
-            swap(r, 1 - core).wait_recv()
-            project_back(r)
-
-            @pl.when(it < NZ + 8)
-            def _():
-                forward(it - NZ - 4)
-
-    @pl.loop(0, NZ)
-    def _(r):
-        lend(r).wait_recv()
-        share(r, core).start()
-
-    @pl.loop(0, 4)
-    def _(n):
-        backward(n)
-
-    @pl.loop(0, 4)
-    def _(n):
-        hand_over(1, n).start()
-
-    @pl.loop(0, 4)
-    def _(n):
-        hand_over(2, n).start()
-
-    @pl.loop(NZ, ROUNDS)
-    def _(r):
-        lend(r).start()
-
-    @pl.loop(0, NZ)
-    def _(r):
-        share(r, 1 - core).wait_recv()
-
 
     def term(g, to_z):
         a = g // 3
@@ -325,19 +251,55 @@
         other = extra[a, :, :, :, other_cols].reshape(2 * PATCH, SPAN)
         return dot(bt[0, here, :], own, ((1,), (0,))) + dot(bt[1, here, :], other, ((1,), (0,)))
 
-    def pass_on(side, s, g, h):
-        source = first.at[sums(g, h)] if s == 0 else run.at[side, s - 1, sums(g, h)]
+    def chain(side, s, g, h):
+        dp_to = ((z + jnp.where(side == 0, 1, 7)) % NZ) * 2 + yh
         return remote(
-            source, run.at[side, s, sums(g, h)],
-            r_send.at[side, s, g * 2 + h], r_recv.at[side, s, g * 2 + h], sides[side],
+            run.at[side, s - 1, sums(g, h)], run.at[side, s, sums(g, h)],
+            r_send.at[side, s, g * 2 + h], r_recv.at[side, s, g * 2 + h], (dp_to, mp),
         )
+
+    def chain_start(side, g, h):
+        return remote(
+            first.at[sums(g, h)], run.at[side, 0, sums(g, h)],
+            r_send.at[side, 0, g * 2 + h], r_recv.at[side, 0, g * 2 + h], sides[side],
+        )
+
+    def chain_landed(side, s, g, h):
+        part = run.at[side, s, sums(g, h)]
+        remote(
+            part, part, r_send.at[side, s, g * 2 + h], r_recv.at[side, s, g * 2 + h], up
+        ).wait_recv()
+
+    def begin(g):
+        part = term(g, (z + 4) % NZ)
+        for h in range(2):
+            first[sums(g, h)] = part[h * HD : (h + 1) * HD].astype(BF16)
+            chain_start(h, g, h).start()
+
+    def advance(g, side, s):
+        part = term(g, (z + jnp.where(side == 0, 4 - s, 4 + s)) % NZ)
+        for h in range(2):
+            piece = part[h * HD : (h + 1) * HD]
+            arrives = (s > 1) | (side == h)
+
+            @pl.when(arrives)
+            def _():
+                chain_landed(side, s - 1, g, h)
+                here = run[side, s - 1, sums(g, h)].astype(F32)
+                run[side, s - 1, sums(g, h)] = (piece + here).astype(BF16)
+
+            @pl.when(jnp.logical_not(arrives))
+            def _():
+                run[side, s - 1, sums(g, h)] = piece.astype(BF16)
+
+            chain(side, s, g, h).start()
 
     def finish(g):
         total = term(g, z)
         for h in range(2):
             part = total[h * HD : (h + 1) * HD]
             for side in range(2):
-                pass_on(side, 3, g, h).wait_recv()
+                chain_landed(side, 3, g, h)
                 part = part + run[side, 3, sums(g, h)].astype(F32)
             done = part.T.astype(BF16)
 
@@ -349,46 +311,174 @@
             def _():
                 oc_ref[:, h * HD : (h + 1) * HD] = done
 
+
+    def stage(it, lag, least=0, most=ROUNDS):
+        return pl.when((it - lag >= least) & (it - lag < most))
+
+    weights_across().start()
+    send_weights(0)
+
+    @pl.loop(0, ROUNDS + 12)
+    def _(it):
+        @stage(it, 0)
+        def _():
+            move(it, 0, x, yl, pair).start()
+            move(it, 1, x, yl, right).start()
+            move(it, 2, x, yl, left).start()
+
+        for m, when in ((1, 2), (2, 4), (3, 5), (4, 7), (5, 9), (6, 11)):
+
+            @pl.when(it == when)
+            def _(m=m):
+                send_weights(m)
+
+        @stage(it, 6)
+        def _():
+            r = it - 6
+            landed(r, 3, left_x, 1 - yl)
+            landed(r, 4, right_x, 1 - yl)
+            landed(r, 6, far_x, 1 - yl)
+            swap(r, core).start()
+
+        @stage(it, 4)
+        def _():
+            r = it - 4
+            landed(r, 5, far_x, yl)
+            move(r, 6, far_x, yl, pair).start()
+
+        @stage(it, 2)
+        def _():
+            r = it - 2
+            landed(r, 0, x, 1 - yl)
+            move(r, 3, x, 1 - yl, right).start()
+            move(r, 4, x, 1 - yl, left).start()
+            landed(r, 1, left_x, yl)
+            landed(r, 2, right_x, yl)
+            onward = place(z, yh, jnp.where(core == 0, right_x, left_x), yl, core)
+            move(r, 5, jnp.where(core == 0, left_x, right_x), yl, onward).start()
+
+        @stage(it, 3, NZ)
+        def _():
+            give(it - 3).start()
+
+        @stage(it, 5, NZ)
+        def _():
+            r = it - 5
+            give(r).wait_recv()
+            pass_quarter(r, 10, x, right).start()
+            pass_quarter(r, 11, x, left).start()
+
+        @stage(it, 7, NZ)
+        def _():
+            r = it - 7
+            pass_quarter(r, 10, left_x, right).wait_recv()
+            pass_quarter(r, 11, right_x, left).wait_recv()
+            onward = place(z, yh, jnp.where(core == 0, right_x, left_x), yl, core)
+            pass_quarter(r, 12, jnp.where(core == 0, left_x, right_x), onward).start()
+
+        @stage(it, 9, NZ)
+        def _():
+            r = it - 9
+            pass_quarter(r, 12, far_x, right).wait_recv()
+            swap_quarters(r, core).start()
+
+        @pl.when((it >= 8) & (it < 24) & (it % 2 == 0))
+        def _():
+            lend((it - 8) // 2).start()
+
+        @pl.when((it >= 11) & (it < 27) & (it % 2 == 1))
+        def _():
+            r = (it - 11) // 2
+            lend(r).wait_recv()
+            share(r, core).start()
+
+        @pl.when(it == 7)
+        def _():
+            loads[3].wait()
+
+        @pl.when(it == 15)
+        def _():
+            weights_landed(6)
+
+        @stage(it, 7)
+        def _():
+            swap(it - 7, 1 - core).wait_recv()
+
+        @stage(it, 7, 0, NZ)
+        def _():
+            project(it - 7)
+
+        @stage(it, 7, NZ)
+        def _():
+            project_back(it - 7)
+
+        @stage(it, 15, 0, 4)
+        def _():
+            forward(it - 15)
+
+        @stage(it, 23, 0, 4)
+        def _():
+            backward(it - 23)
+
+        @pl.when(it == 20)
+        def _():
+            for n in range(4):
+                hand_over(3, n).wait_recv()
+
+        @stage(it, 12, NZ)
+        def _():
+            r = it - 12
+            j = r - NZ
+            swap_quarters(r, 1 - core).wait_recv()
+
+            @pl.when(j == 0)
+            def _():
+                begin(3)
+
+            @pl.when((j > 0) & (j < 7))
+            def _():
+                advance(3, 1 - j % 2, (j + 1) // 2)
+
     @pl.loop(0, 4)
-    def _(g):
-        @pl.when(g == 3)
-        def _():
-            @pl.loop(NZ, ROUNDS)
-            def _(r):
-                share(r, 1 - core).wait_recv()
-
-        @pl.loop(0, 4)
-        def _(n):
-            hand_over(g, n).wait_recv()
-
-        start = term(g, (z + 4) % NZ)
-        for h in range(2):
-            first[sums(g, h)] = start[h * HD : (h + 1) * HD].astype(BF16)
-            pass_on(h, 0, g, h).start()
-        for s in range(1, 4):
-            for side in range(2):
-                part = term(g, (z + (4 - s if side == 0 else 4 + s)) % NZ)
-                for h in (0, 1) if (s > 1 or side == 1) else (1, 0):
-                    piece = part[h * HD : (h + 1) * HD]
-                    if s > 1 or h == side:
-                        pass_on(side, s - 1, g, h).wait_recv()
-                        piece = piece + run[side, s - 1, sums(g, h)].astype(F32)
-                    run[side, s - 1, sums(g, h)] = piece.astype(BF16)
-                    pass_on(side, s, g, h).start()
-            if s == 1:
-
-                @pl.when(g > 0)
-                def _():
-                    finish(g - 1)
-
-        @pl.when(g == 1)
-        def _():
-            @pl.loop(NZ, ROUNDS)
-            def _(r):
-                lend(r).wait_recv()
-                share(r, core).start()
-
-    finish(3)
+    def _(n):
+        hand_over(1, n).start()
+
+    @pl.loop(0, 4)
+    def _(n):
+        hand_over(2, n).start()
+
+    @pl.loop(0, NZ)
+    def _(r):
+        share(r, 1 - core).wait_recv()
+
+    def pick(t, table):
+        return sum(jnp.where(t == i, v, 0) for i, v in enumerate(table) if v)
+
+    plan = (
+        (0, 0), (0, 1), (1, 0), (0, 2), (1, 1), (0, 3), (3, 4), (1, 2), (2, 0), (0, 4),
+        (1, 3), (2, 1), (1, 4), (2, 2), (2, 3), (2, 4),
+    )
+
+    @pl.loop(0, len(plan))
+    def _(t):
+        g = pick(t, [g for g, _ in plan])
+        s = pick(t, [s for _, s in plan])
+
+        @pl.when(s == 0)
+        def _():
+            for n in range(4):
+                hand_over(g, n).wait_recv()
+            begin(g)
+
+        @pl.when((s > 0) & (s < 4))
+        def _():
+            @pl.loop(0, 2)
+            def _(side):
+                advance(g, side, s)
+
+        @pl.when(s == 4)
+        def _():
+            finish(g)
 
 
     weights_across().wait_send()
@@ -401,18 +491,28 @@
         for slot in range(7):
             move(r, slot, x, yl, pair).wait_send()
         swap(r, core).wait_send()
+
+    @pl.loop(0, NZ)
+    def _(r):
         lend(r).wait_send()
         share(r, core).wait_send()
+
+    @pl.loop(NZ, ROUNDS)
+    def _(r):
+        give(r).wait_send()
+        for slot in range(10, 13):
+            pass_quarter(r, slot, x, right).wait_send()
+        swap_quarters(r, core).wait_send()
 
     @pl.loop(0, 4)
     def _(g):
         for n in range(4):
             hand_over(g, n).wait_send()
         for side in range(2):
-            for s in range(4):
+            chain_start(side, g, side).wait_send()
+            for s in range(1, 4):
                 for h in range(2):
-                    if s > 0 or h == side:
-                        pass_on(side, s, g, h).wait_send()
+                    chain(side, s, g, h).wait_send()
 
 
 def body(tokens, w_qkv, w_out, grad_out):
@@ -440,7 +540,7 @@
             vmem((2, 4, 8 * HD, SPAN), BF16),
             vmem((8 * HD, SPAN), BF16),
             dma((4,)),
-            dma((ROUNDS, 10)), dma((ROUNDS, 10)),
+            dma((ROUNDS, 13)), dma((ROUNDS, 13)),
             dma((2, 7)), dma((2, 7)),
             dma((1,)), dma((1,)),
             dma((4, 4)), dma((4, 4)),

time: 177 us -> 153 us (0.86)
  Pallas kernels: 172 us -> 148 us
    pallas_call x1, Pallas kernels: 172 us -> 148 us  [body(): pl.pallas_call(kernel, out_shape=(jax.ShapeDtypeStruct((SPAN, 6 * HD), BF...]
where the time goes in v2:
time: 153 us
  Pallas kernels  148 us (97%)
  local copies, waits for them, and re-layouts  4.16 us (3%)
    pallas_call x1, Pallas kernels, body(): pl.pallas_call(kernel, out_shape=(jax.ShapeDtypeStruct((SPAN, 6 * HD), BF...  148 us
    reshape x2, local copies, waits for them, and re-layouts, body(): return (grad_qkv.reshape(SPAN, 2, 3 * HD), grad_wo.reshape(SPAN, 2, HD))  4.16 us

profile of v2, /device:TPU:8, one launch (start us, length us, event | category | flops | bytes accessed | tf_op | source)
XLA Modules:
  0.0 153.0 jit_solution(2936708619732994438)
XLA Ops:
  0.6 148.2 %shard_map.59 = (bf16[384,768]{1,0:T(8,128)(2,1)}, bf16[384,256]{1,0:T(8,128)(2,1)}) custom-call(bf16[32,6144]{1,0:T(8,128)(2,1)} %tok_ref.1, bf16[6144,2,384]{2,1,0:T(2,128)(2,1)} %wq_ref.1, bf16[384,2,128]{2,1,0:T(2,128)(2,1)} %wo_ref.1, bf16[32,6144]{1,0:T(8,128)(2,1)} %go_ref.1), custom_call_target="tpu_custom_call" | custom-call | tf_op jit(solution)/shard_map/pallas_call | solution.py:521
  148.9 2.5 %reshape.10 = bf16[384,2,384]{2,1,0:T(2,128)(2,1)} reshape(bf16[384,768]{1,0:T(8,128)(2,1)} %get-tuple-element.4) | data formatting | bytes 1179648 | tf_op jit(solution)/shard_map/reshape | solution.py:553
  151.4 1.7 %reshape.11 = bf16[384,2,128]{2,1,0:T(2,128)(2,1)} reshape(bf16[384,256]{1,0:T(8,128)(2,1)} %get-tuple-element.5) | data formatting | bytes 393216 | tf_op jit(solution)/shard_map/reshape | solution.py:553

commit v3 on v2

--- a/solution.py
+++ b/solution.py
@@ -41,7 +41,7 @@
     tok_ref, wq_ref, wo_ref, go_ref,
     oq_ref, oc_ref,
     rows, extra, wq, wo, wpart, proj, gctx, hats, chances, bt, run, first,
-    local, g_send, g_recv, w_send, w_recv, y_send, y_recv, b_send, b_recv, r_send, r_recv,
+    local, sent, g_recv, w_recv, y_recv, b_recv, r_recv,
 ):
     dp, mp = lax.axis_index("dp"), lax.axis_index("mp")
     z, yh = dp // 2, dp % 2
@@ -99,14 +99,14 @@
 
     def move(r, slot, bx, by, to):
         part = block(r, bx, by)
-        return remote(part, part, g_send.at[r, slot], g_recv.at[r, slot], to)
+        return remote(part, part, sent.at[0], g_recv.at[r, slot], to)
 
     def landed(r, slot, bx, by):
         move(r, slot, bx, by, pair).wait_recv()
 
     def swap(r, lane):
         part = rows.at[r // NZ, :, lane, :, columns(r)]
-        return remote(part, part, g_send.at[r, 7], g_recv.at[r, 7], sibling)
+        return remote(part, part, sent.at[1], g_recv.at[r, 7], sibling)
 
     def lend(r):
         cols = pl.ds(pl.multiple_of(target(r) * PAIR + (1 - yh) * SPAN, SPAN), SPAN)
@@ -114,13 +114,13 @@
         half = pl.ds(core * 4, 4)
         return remote(
             rows.at[0, half, :, :, cols], extra.at[0, half, :, :, there],
-            g_send.at[r, 8], g_recv.at[r, 8], outer,
+            sent.at[2], g_recv.at[r, 8], outer,
         )
 
     def share(r, owner):
         there = pl.ds(pl.multiple_of(target(r) * SPAN, SPAN), SPAN)
         part = extra.at[0, pl.ds(owner * 4, 4), :, :, there]
-        return remote(part, part, g_send.at[r, 9], g_recv.at[r, 9], sibling)
+        return remote(part, part, sent.at[3], g_recv.at[r, 9], sibling)
 
     def quarter(r, bx):
         there = pl.ds(pl.multiple_of(target(r) * SPAN, SPAN), SPAN)
@@ -129,16 +129,16 @@
     def give(r):
         cols = pl.ds(pl.multiple_of(target(r) * PAIR + (1 - yh) * SPAN, SPAN), SPAN)
         mine = rows.at[1, pl.ds(x * 2, 2), core, :, cols]
-        return remote(mine, quarter(r, x), g_send.at[r, 8], g_recv.at[r, 8], outer)
+        return remote(mine, quarter(r, x), sent.at[4], g_recv.at[r, 8], outer)
 
     def pass_quarter(r, slot, bx, to):
         part = quarter(r, bx)
-        return remote(part, part, g_send.at[r, slot], g_recv.at[r, slot], to)
+        return remote(part, part, sent.at[5], g_recv.at[r, slot], to)
 
     def swap_quarters(r, lane):
         there = pl.ds(pl.multiple_of(target(r) * SPAN, SPAN), SPAN)
         part = extra.at[1, :, lane, :, there]
-        return remote(part, part, g_send.at[r, 9], g_recv.at[r, 9], sibling)
+        return remote(part, part, sent.at[6], g_recv.at[r, 9], sibling)
 
 
     def weights(side, m):
@@ -146,7 +146,7 @@
         from_z = (z + (NZ - hop if side == 0 else hop)) % NZ
         own = (m % 2 == 0) if (m < 6 or side == 0) else False
         part = wo.at[from_z, yh if own else 1 - yh]
-        return remote(part, part, w_send.at[side, m], w_recv.at[side, m], sides[side])
+        return remote(part, part, sent.at[7], w_recv.at[side, m], sides[side])
 
     def weights_landed(m):
         for side in range(2):
@@ -154,7 +154,7 @@
 
     def weights_across():
         part = wo.at[z, yh]
-        return remote(part, part, y_send.at[0], y_recv.at[0], across)
+        return remote(part, part, sent.at[8], y_recv.at[0], across)
 
     def send_weights(m):
         if m == 1:
@@ -180,7 +180,7 @@
         i, h = n // 2, n % 2
         return remote(
             bt.at[0, sums(g, h), image_rows(i)], bt.at[1, sums(g, h), image_rows(i)],
-            b_send.at[g, n], b_recv.at[g, n], across,
+            sent.at[9], b_recv.at[g, n], across,
         )
 
     def forward(n):
@@ -255,19 +255,19 @@
         dp_to = ((z + jnp.where(side == 0, 1, 7)) % NZ) * 2 + yh
         return remote(
             run.at[side, s - 1, sums(g, h)], run.at[side, s, sums(g, h)],
-            r_send.at[side, s, g * 2 + h], r_recv.at[side, s, g * 2 + h], (dp_to, mp),
+            sent.at[10], r_recv.at[side, s, g * 2 + h], (dp_to, mp),
         )
 
     def chain_start(side, g, h):
         return remote(
             first.at[sums(g, h)], run.at[side, 0, sums(g, h)],
-            r_send.at[side, 0, g * 2 + h], r_recv.at[side, 0, g * 2 + h], sides[side],
+            sent.at[10], r_recv.at[side, 0, g * 2 + h], sides[side],
         )
 
     def chain_landed(side, s, g, h):
         part = run.at[side, s, sums(g, h)]
         remote(
-            part, part, r_send.at[side, s, g * 2 + h], r_recv.at[side, s, g * 2 + h], up
+            part, part, sent.at[10], r_recv.at[side, s, g * 2 + h], up
         ).wait_recv()
 
     def begin(g):
@@ -318,7 +318,7 @@
     weights_across().start()
     send_weights(0)
 
-    @pl.loop(0, ROUNDS + 12)
+    @pl.loop(0, ROUNDS + 11)
     def _(it):
         @stage(it, 0)
         def _():
@@ -420,14 +420,14 @@
         def _():
             backward(it - 23)
 
-        @pl.when(it == 20)
+        @pl.when(it == 19)
         def _():
             for n in range(4):
                 hand_over(3, n).wait_recv()
 
-        @stage(it, 12, NZ)
-        def _():
-            r = it - 12
+        @stage(it, 11, NZ)
+        def _():
+            r = it - 11
             j = r - NZ
             swap_quarters(r, 1 - core).wait_recv()
 
@@ -481,38 +481,29 @@
             finish(g)
 
 
-    weights_across().wait_send()
-    for side in range(2):
-        for m in range(7):
-            weights(side, m).wait_send()
-
-    @pl.loop(0, ROUNDS)
-    def _(r):
-        for slot in range(7):
-            move(r, slot, x, yl, pair).wait_send()
-        swap(r, core).wait_send()
-
-    @pl.loop(0, NZ)
-    def _(r):
-        lend(r).wait_send()
-        share(r, core).wait_send()
-
-    @pl.loop(NZ, ROUNDS)
-    def _(r):
-        give(r).wait_send()
-        for slot in range(10, 13):
-            pass_quarter(r, slot, x, right).wait_send()
-        swap_quarters(r, core).wait_send()
-
-    @pl.loop(0, 4)
-    def _(g):
-        for n in range(4):
-            hand_over(g, n).wait_send()
-        for side in range(2):
-            chain_start(side, g, side).wait_send()
-            for s in range(1, 4):
-                for h in range(2):
-                    chain(side, s, g, h).wait_send()
+    gone = (
+        rows.at[:, pl.ds(0, 7), core],
+        rows.at[:, :, core],
+        extra.at[0, pl.ds(0, 4)],
+        extra.at[0, pl.ds(0, 4)],
+        extra.at[1, pl.ds(0, 2), core],
+        extra.at[1, pl.ds(0, 6), core],
+        extra.at[1, :, core],
+        wo.at[pl.ds(0, 7)],
+        wo.at[0, 0],
+        bt.at[0],
+        run.at[:, :, pl.ds(0, 7 * HD)],
+    )
+    for kind, part in enumerate(gone):
+        remote(part, part, sent.at[kind], y_recv.at[0], up).wait_send()
+
+
+def split_heads(qkv_ref, out_ref, qkv_heads_ref, out_heads_ref):
+    @pl.loop(0, SPAN // HD)
+    def _(k):
+        here = pl.ds(pl.multiple_of(k * HD, HD), HD)
+        qkv_heads_ref[here] = qkv_ref[here].reshape(HD, 2, 3 * HD)
+        out_heads_ref[here] = out_ref[here].reshape(HD, 2, HD)
 
 
 def body(tokens, w_qkv, w_out, grad_out):
@@ -540,17 +531,26 @@
             vmem((2, 4, 8 * HD, SPAN), BF16),
             vmem((8 * HD, SPAN), BF16),
             dma((4,)),
-            dma((ROUNDS, 13)), dma((ROUNDS, 13)),
-            dma((2, 7)), dma((2, 7)),
-            dma((1,)), dma((1,)),
-            dma((4, 4)), dma((4, 4)),
-            dma((2, 4, 8)), dma((2, 4, 8)),
+            dma((11,)),
+            dma((ROUNDS, 13)),
+            dma((2, 7)),
+            dma((1,)),
+            dma((4, 4)),
+            dma((2, 4, 8)),
         ],
         compiler_params=pltpu.CompilerParams(
             collective_id=0, has_side_effects=True, vmem_limit_bytes=60 << 20
         ),
     )(tokens, w_qkv, w_out, grad_out)
-    return grad_qkv.reshape(SPAN, 2, 3 * HD), grad_wo.reshape(SPAN, 2, HD)
+    return pl.pallas_call(
+        split_heads,
+        out_shape=(
+            jax.ShapeDtypeStruct((SPAN, 2, 3 * HD), BF16),
+            jax.ShapeDtypeStruct((SPAN, 2, HD), BF16),
+        ),
+        in_specs=[pl.BlockSpec(memory_space=vmem)] * 2,
+        out_specs=(pl.BlockSpec(memory_space=vmem), pl.BlockSpec(memory_space=vmem)),
+    )(grad_qkv, grad_wo)
 
 
 def solution(mesh):

time: 153 us -> 148 us (0.967)
  local copies, waits for them, and re-layouts: 4.16 us -> 0 us
    reshape x2 -> x0, local copies, waits for them, and re-layouts: 4.16 us -> none  [body(): return (grad_qkv.reshape(SPAN, 2, 3 * HD), grad_wo.reshape(SPAN, 2, HD))]
    pallas_call x1, Pallas kernels: 148 us -> 144 us  [body(): pl.pallas_call(kernel, out_shape=(jax.ShapeDtypeStruct((SPAN, 6 * HD), BF...]
    pallas_call x0 -> x1, Pallas kernels: none -> 2.48 us  [body(): pl.pallas_call(split_heads, out_shape=(jax.ShapeDtypeStruct((SPAN, 2, 3 *...]
where the time goes in v3:
time: 148 us; the launch traced here: 147 us
  Pallas kernels  147 us (99%)
    pallas_call x1, Pallas kernels, body(): pl.pallas_call(kernel, out_shape=(jax.ShapeDtypeStruct((SPAN, 6 * HD), BF...  144 us

profile of v3, /device:TPU:8, one launch (start us, length us, event | category | flops | bytes accessed | tf_op | source)
XLA Modules:
  0.0 147.4 jit_solution(12273430681795566718)
XLA Ops:
  0.6 144.3 %shard_map.59 = (bf16[384,768]{1,0:T(8,128)(2,1)}, bf16[384,256]{1,0:T(8,128)(2,1)}) custom-call(bf16[32,6144]{1,0:T(8,128)(2,1)} %tok_ref.1, bf16[6144,2,384]{2,1,0:T(2,128)(2,1)} %wq_ref.1, bf16[384,2,128]{2,1,0:T(2,128)(2,1)} %wo_ref.1, bf16[32,6144]{1,0:T(8,128)(2,1)} %go_ref.1), custom_call_target="tpu_custom_call" | custom-call | tf_op jit(solution)/shard_map/pallas_call | solution.py:512
  144.9 2.5 %shard_map.60 = (bf16[384,2,384]{2,1,0:T(2,128)(2,1)}, bf16[384,2,128]{2,1,0:T(2,128)(2,1)}) custom-call(bf16[384,768]{1,0:T(8,128)(2,1)} %get-tuple-element.4.qkv_ref, bf16[384,256]{1,0:T(8,128)(2,1)} %get-tuple-element.5.out_ref), custom_call_target="tpu_custom_call" | custom-call | tf_op jit(solution)/shard_map/pallas_call | solution.py:545

commit v4 on v3

--- a/solution.py
+++ b/solution.py
@@ -16,6 +16,7 @@
 SPAN = 384
 PAIR = 2 * SPAN
 ROUNDS = 2 * NZ
+ARRIVES = {0: 0, 1: 1, 2: 1, 3: 2, 4: 2, 5: 3, 6: 2, 10: 7, 11: 7, 12: 8}
 HD = 128
 EPS = 1e-06
 FACTOR = HD ** (-0.5)
@@ -99,14 +100,18 @@
 
     def move(r, slot, bx, by, to):
         part = block(r, bx, by)
-        return remote(part, part, sent.at[0], g_recv.at[r, slot], to)
+        return remote(part, part, sent.at[0], g_recv.at[r, ARRIVES[slot]], to)
 
     def landed(r, slot, bx, by):
         move(r, slot, bx, by, pair).wait_recv()
 
+    def landed_all(r, slot, count):
+        part = rows.at[r // NZ, pl.ds(0, count), core, :, columns(r)]
+        remote(part, part, sent.at[0], g_recv.at[r, ARRIVES[slot]], pair).wait_recv()
+
     def swap(r, lane):
         part = rows.at[r // NZ, :, lane, :, columns(r)]
-        return remote(part, part, sent.at[1], g_recv.at[r, 7], sibling)
+        return remote(part, part, sent.at[1], g_recv.at[r, 4], sibling)
 
     def lend(r):
         cols = pl.ds(pl.multiple_of(target(r) * PAIR + (1 - yh) * SPAN, SPAN), SPAN)
@@ -114,13 +119,13 @@
         half = pl.ds(core * 4, 4)
         return remote(
             rows.at[0, half, :, :, cols], extra.at[0, half, :, :, there],
-            sent.at[2], g_recv.at[r, 8], outer,
+            sent.at[2], g_recv.at[r, 5], outer,
         )
 
     def share(r, owner):
         there = pl.ds(pl.multiple_of(target(r) * SPAN, SPAN), SPAN)
         part = extra.at[0, pl.ds(owner * 4, 4), :, :, there]
-        return remote(part, part, sent.at[3], g_recv.at[r, 9], sibling)
+        return remote(part, part, sent.at[3], g_recv.at[r, 6], sibling)
 
     def quarter(r, bx):
         there = pl.ds(pl.multiple_of(target(r) * SPAN, SPAN), SPAN)
@@ -129,16 +134,16 @@
     def give(r):
         cols = pl.ds(pl.multiple_of(target(r) * PAIR + (1 - yh) * SPAN, SPAN), SPAN)
         mine = rows.at[1, pl.ds(x * 2, 2), core, :, cols]
-        return remote(mine, quarter(r, x), sent.at[4], g_recv.at[r, 8], outer)
+        return remote(mine, quarter(r, x), sent.at[4], g_recv.at[r, 5], outer)
 
     def pass_quarter(r, slot, bx, to):
         part = quarter(r, bx)
-        return remote(part, part, sent.at[5], g_recv.at[r, slot], to)
+        return remote(part, part, sent.at[5], g_recv.at[r, ARRIVES[slot]], to)
 
     def swap_quarters(r, lane):
         there = pl.ds(pl.multiple_of(target(r) * SPAN, SPAN), SPAN)
         part = extra.at[1, :, lane, :, there]
-        return remote(part, part, sent.at[6], g_recv.at[r, 9], sibling)
+        return remote(part, part, sent.at[6], g_recv.at[r, 6], sibling)
 
 
     def weights(side, m):
@@ -332,12 +337,14 @@
             def _(m=m):
                 send_weights(m)
 
+        @stage(it, 23, 0, 4)
+        def _():
+            backward(it - 23)
+
         @stage(it, 6)
         def _():
             r = it - 6
-            landed(r, 3, left_x, 1 - yl)
-            landed(r, 4, right_x, 1 - yl)
-            landed(r, 6, far_x, 1 - yl)
+            landed_all(r, 3, 3)
             swap(r, core).start()
 
         @stage(it, 4)
@@ -352,8 +359,7 @@
             landed(r, 0, x, 1 - yl)
             move(r, 3, x, 1 - yl, right).start()
             move(r, 4, x, 1 - yl, left).start()
-            landed(r, 1, left_x, yl)
-            landed(r, 2, right_x, yl)
+            landed_all(r, 1, 2)
             onward = place(z, yh, jnp.where(core == 0, right_x, left_x), yl, core)
             move(r, 5, jnp.where(core == 0, left_x, right_x), yl, onward).start()
 
@@ -371,8 +377,9 @@
         @stage(it, 7, NZ)
         def _():
             r = it - 7
-            pass_quarter(r, 10, left_x, right).wait_recv()
-            pass_quarter(r, 11, right_x, left).wait_recv()
+            there = pl.ds(pl.multiple_of(target(r) * SPAN, SPAN), SPAN)
+            both = extra.at[1, pl.ds(0, 4), core, :, there]
+            remote(both, both, sent.at[5], g_recv.at[r, 7], right).wait_recv()
             onward = place(z, yh, jnp.where(core == 0, right_x, left_x), yl, core)
             pass_quarter(r, 12, jnp.where(core == 0, left_x, right_x), onward).start()
 
@@ -415,10 +422,6 @@
         @stage(it, 15, 0, 4)
         def _():
             forward(it - 15)
-
-        @stage(it, 23, 0, 4)
-        def _():
-            backward(it - 23)
 
         @pl.when(it == 19)
         def _():
@@ -532,7 +535,7 @@
             vmem((8 * HD, SPAN), BF16),
             dma((4,)),
             dma((11,)),
-            dma((ROUNDS, 13)),
+            dma((ROUNDS, 9)),
             dma((2, 7)),
             dma((1,)),
             dma((4, 4)),

time: 148 us -> 147 us (level)
  no operation moved by 1% of the time
where the time goes in v4:
time: 147 us; the launch traced here: 146 us
  Pallas kernels  146 us (99%)
    pallas_call x1, Pallas kernels, body(): pl.pallas_call(kernel, out_shape=(jax.ShapeDtypeStruct((SPAN, 6 * HD), BF...  143 us

profile of v4, /device:TPU:8, one launch (start us, length us, event | category | flops | bytes accessed | tf_op | source)
XLA Modules:
  0.0 146.5 jit_solution(18212400886316212915)
XLA Ops:
  0.6 143.4 %shard_map.59 = (bf16[384,768]{1,0:T(8,128)(2,1)}, bf16[384,256]{1,0:T(8,128)(2,1)}) custom-call(bf16[32,6144]{1,0:T(8,128)(2,1)} %tok_ref.1, bf16[6144,2,384]{2,1,0:T(2,128)(2,1)} %wq_ref.1, bf16[384,2,128]{2,1,0:T(2,128)(2,1)} %wo_ref.1, bf16[32,6144]{1,0:T(8,128)(2,1)} %go_ref.1), custom_call_target="tpu_custom_call" | custom-call | tf_op jit(solution)/shard_map/pallas_call | solution.py:515
  144.0 2.5 %shard_map.60 = (bf16[384,2,384]{2,1,0:T(2,128)(2,1)}, bf16[384,2,128]{2,1,0:T(2,128)(2,1)}) custom-call(bf16[384,768]{1,0:T(8,128)(2,1)} %get-tuple-element.4.qkv_ref, bf16[384,256]{1,0:T(8,128)(2,1)} %get-tuple-element.5.out_ref), custom_call_target="tpu_custom_call" | custom-call | tf_op jit(solution)/shard_map/pallas_call | solution.py:548

commit v5 on v4

--- a/solution.py
+++ b/solution.py
@@ -458,8 +458,8 @@
         return sum(jnp.where(t == i, v, 0) for i, v in enumerate(table) if v)
 
     plan = (
-        (0, 0), (0, 1), (1, 0), (0, 2), (1, 1), (0, 3), (3, 4), (1, 2), (2, 0), (0, 4),
-        (1, 3), (2, 1), (1, 4), (2, 2), (2, 3), (2, 4),
+        (0, 0), (0, 1), (1, 0), (0, 2), (2, 0), (1, 1), (0, 3), (3, 4), (2, 1), (1, 2), (0, 4),
+        (2, 2), (1, 3), (2, 3), (1, 4), (2, 4),
     )
 
     @pl.loop(0, len(plan))

time: 147 us -> 144 us (0.980)
  Pallas kernels: 146 us -> 143 us
    pallas_call x1, Pallas kernels: 143 us -> 140 us  [body(): pl.pallas_call(kernel, out_shape=(jax.ShapeDtypeStruct((SPAN, 6 * HD), BF...]
where the time goes in v5:
time: 144 us; the launch traced here: 143 us
  Pallas kernels  143 us (99%)
    pallas_call x1, Pallas kernels, body(): pl.pallas_call(kernel, out_shape=(jax.ShapeDtypeStruct((SPAN, 6 * HD), BF...  140 us

profile of v5, /device:TPU:8, one launch (start us, length us, event | category | flops | bytes accessed | tf_op | source)
XLA Modules:
  0.0 143.4 jit_solution(12850998175954848251)
XLA Ops:
  0.6 140.3 %shard_map.59 = (bf16[384,768]{1,0:T(8,128)(2,1)}, bf16[384,256]{1,0:T(8,128)(2,1)}) custom-call(bf16[32,6144]{1,0:T(8,128)(2,1)} %tok_ref.1, bf16[6144,2,384]{2,1,0:T(2,128)(2,1)} %wq_ref.1, bf16[384,2,128]{2,1,0:T(2,128)(2,1)} %wo_ref.1, bf16[32,6144]{1,0:T(8,128)(2,1)} %go_ref.1), custom_call_target="tpu_custom_call" | custom-call | tf_op jit(solution)/shard_map/pallas_call | solution.py:515
  141.0 2.5 %shard_map.60 = (bf16[384,2,384]{2,1,0:T(2,128)(2,1)}, bf16[384,2,128]{2,1,0:T(2,128)(2,1)}) custom-call(bf16[384,768]{1,0:T(8,128)(2,1)} %get-tuple-element.4.qkv_ref, bf16[384,256]{1,0:T(8,128)(2,1)} %get-tuple-element.5.out_ref), custom_call_target="tpu_custom_call" | custom-call | tf_op jit(solution)/shard_map/pallas_call | solution.py:548
